TPU v7x, 768 devices: a whole 4x8x12 slice. The times are simulated.
768 devices in a mesh: seq: 16 (over x, y_hi, core), head: 12 (over z), rep: 4 (over y_lo).
Axes of the slice: x: 4, y: 8 (y_hi: 2, y_lo: 4; y = y_hi * 4 + y_lo), z: 12, core: 2. Of those that a mesh axis runs over, the one named last changes fastest.
Arguments:
- queries: bfloat16 [64, 1536, 3072], P(('seq', 'rep'), 'head'), may hold values from -18 to 18, as said below
- keys: bfloat16 [64, 1536, 3072], P(('seq', 'rep'), 'head'), may hold values from -18 to 18, as said below
- values: bfloat16 [64, 1536, 3072], P(('seq', 'rep'), 'head'), may hold values from -6 to 6
- text_kv: bfloat16 [64, 384, 6144], P(('seq', 'rep'), 'head'), may hold values from -18 to 18, as said below
- cotangent: bfloat16 [64, 1536, 3072], P(('seq', 'rep'), None, 'head'), may hold values from -6 to 6
Outputs:
- attended: bfloat16 [64, 1536, 3072], P(('seq', 'rep'), None, 'head')
- text_grad: bfloat16 [64, 384, 6144], P(('seq', 'rep'), 'head')
Inputs may be any that keep to these rules, and one draw needn't show every extreme that they name: `queries`: normal-like entries of order one. `keys`: normal-like entries of order one. `text_kv`: normal-like entries of order one.
All inputs are finite; a program needn't handle non-finite values.
Results may differ from a plain program's by a relative error of at most 0.007.
Values may be sent and summed in bfloat16 or wider, within the bound.
A program may use at most 32 MiB of HBM per device.

v0:
```python
import jax
import jax.numpy as jnp
from jax import lax
from jax.sharding import PartitionSpec as P

HD = 128


def softmax_rows(scores):
    top = jnp.max(scores, axis=-1, keepdims=True)
    weights = jnp.exp(scores - top)
    return weights / jnp.sum(weights, axis=-1, keepdims=True)


def block_rows():
    return 512


def self_part(query_block, key_all, value_all, scale):
    scores = (
        jnp.einsum("bgd,lgd->gbl", query_block, key_all, preferred_element_type=jnp.float32) * scale
    )
    probs = softmax_rows(scores).astype(jnp.bfloat16)
    return jnp.einsum("gbl,lgd->bgd", probs, value_all, preferred_element_type=jnp.float32)


def cross_part(query_block, grad_block, text_keys, text_values, scale):
    cross_scores = (
        jnp.einsum("bgd,tgd->gbt", query_block, text_keys, preferred_element_type=jnp.float32)
        * scale
    )
    cross_probs = softmax_rows(cross_scores)
    cross_rounded = cross_probs.astype(jnp.bfloat16)
    cross_out = jnp.einsum(
        "gbt,tgd->bgd", cross_rounded, text_values, preferred_element_type=jnp.float32
    )
    grad_values = jnp.einsum(
        "gbt,bgd->tgd", cross_rounded, grad_block, preferred_element_type=jnp.float32
    )
    dprobs = jnp.einsum("bgd,tgd->gbt", grad_block, text_values, preferred_element_type=jnp.float32)
    dscores = cross_probs * (dprobs - jnp.sum(dprobs * cross_probs, axis=-1, keepdims=True))
    dscores = dscores.astype(jnp.bfloat16)
    grad_keys = (
        jnp.einsum("gbt,bgd->tgd", dscores, query_block, preferred_element_type=jnp.float32) * scale
    )
    return (cross_out, grad_keys, grad_values)


def per_device(queries, keys, values, text_kv, cotangent):
    scale = float(HD) ** (-0.5)
    tokens = queries.shape[1]
    heads = queries.shape[2] // HD
    shape_in = (tokens, heads, HD)
    moved_query = lax.all_to_all(
        queries.reshape(shape_in), "head", split_axis=1, concat_axis=0, tiled=True
    )
    text_local = text_kv.reshape(text_kv.shape[1], heads, 2 * HD)
    text_all = lax.all_to_all(text_local, "head", split_axis=1, concat_axis=0, tiled=True)
    moved_key, moved_value = (
        lax.all_to_all(keys.reshape(shape_in), "head", split_axis=1, concat_axis=0, tiled=True),
        lax.all_to_all(values.reshape(shape_in), "head", split_axis=1, concat_axis=0, tiled=True),
    )
    length = moved_query.shape[0]
    groups = moved_query.shape[1]
    text_count = text_all.shape[0]
    text_keys = text_all[:, :, :HD]
    text_values = text_all[:, :, HD:]
    block = block_rows()
    count_blocks = length // block
    query_blocks = moved_query.reshape(count_blocks, block, groups, HD)
    grad_blocks = cotangent.reshape(count_blocks, block, groups, HD)
    zeros = jnp.zeros((text_count, groups, HD), jnp.float32)

    def both_step(totals, pieces):
        cross_out, grad_keys, grad_values = cross_part(
            pieces[0], pieces[1], text_keys, text_values, scale
        )
        self_out = self_part(pieces[0], moved_key, moved_value, scale)
        return (
            (totals[0] + grad_keys, totals[1] + grad_values),
            (self_out + cross_out).astype(jnp.bfloat16),
        )

    (grad_keys, grad_values), outputs = lax.scan(
        both_step, (zeros, zeros), (query_blocks, grad_blocks)
    )
    attended = outputs.reshape(1, length, groups * HD)
    grad_term = (
        jnp.stack([grad_keys, grad_values], axis=2)
        .reshape(text_count, groups, 2 * HD)
        .astype(jnp.bfloat16)
    )
    returned = lax.all_to_all(grad_term, "head", split_axis=0, concat_axis=1, tiled=True)
    return (attended, returned.reshape(1, returned.shape[0], returned.shape[1] * returned.shape[2]))


def solution(mesh):
    placed = (
        P(("seq", "rep"), "head", None),
        P(("seq", "rep"), "head", None),
        P(("seq", "rep"), "head", None),
        P(("seq", "rep"), "head", None),
        P(("seq", "rep"), None, "head"),
    )
    return jax.shard_map(
        per_device,
        mesh=mesh,
        in_specs=placed,
        out_specs=(P(("seq", "rep"), None, "head"), P(("seq", "rep"), "head", None)),
        check_vma=False,
    )
```

profile of v0, /device:TPU:56, one launch (start us, length us, event | category | flops | bytes accessed | tf_op | source)
XLA Modules:
  0.0 244.7 jit_solution(1296816038754732060)
XLA Ops:
  2.6 15.2 %all-to-all-start.1 = ((bf16[32,24,256]{2,0,1:T(8,128)(2,1)}), bf16[32,24,256]{2,0,1:T(8,128)(2,1)S(1)}, u32[]{:S(2)}, u32[]{:S(2)}) async-start(bf16[32,24,256]{2,0,1:T(8,128)(2,1)} %copy.70), calls=%async_computation.1 | async-start | bytes 786432 | tf_op jit(solution)/shard_map/all_to_all | solution.py:58
  19.0 18.6 %all-to-all-done.1 = bf16[32,24,256]{2,0,1:T(8,128)(2,1)S(1)} async-done(((bf16[32,24,256]{2,0,1:T(8,128)(2,1)}), bf16[32,24,256]{2,0,1:T(8,128)(2,1)S(1)}, u32[]{:S(2)}, u32[]{:S(2)}) %all-to-all-start.1) | async-done | bytes 393248 | tf_op jit(solution)/shard_map/all_to_all | solution.py:58
  37.5 3.7 %all-to-all-start.2 = ((bf16[128,24,128]{0,2,1:T(8,128)(2,1)}), bf16[128,24,128]{0,2,1:T(8,128)(2,1)S(1)}, u32[]{:S(2)}, u32[]{:S(2)}) async-start(bf16[128,24,128]{0,2,1:T(8,128)(2,1)} %bitcast.8), calls=%async_computation.2 | async-start | bytes 1572864 | tf_op jit(solution)/shard_map/all_to_all | solution.py:60
  42.4 31.1 %all-to-all-done.2 = bf16[128,24,128]{0,2,1:T(8,128)(2,1)S(1)} async-done(((bf16[128,24,128]{0,2,1:T(8,128)(2,1)}), bf16[128,24,128]{0,2,1:T(8,128)(2,1)S(1)}, u32[]{:S(2)}, u32[]{:S(2)}) %all-to-all-start.2) | async-done | bytes 786464 | tf_op jit(solution)/shard_map/all_to_all | solution.py:60
  73.5 3.6 %all-to-all-start.3 = ((bf16[128,24,128]{0,2,1:T(8,128)(2,1)}), bf16[128,24,128]{0,2,1:T(8,128)(2,1)S(1)}, u32[]{:S(2)}, u32[]{:S(2)}) async-start(bf16[128,24,128]{0,2,1:T(8,128)(2,1)} %bitcast.13), calls=%async_computation.3 | async-start | bytes 1572864 | tf_op jit(solution)/shard_map/all_to_all | solution.py:61
  78.3 30.7 %all-to-all-done.3 = bf16[128,24,128]{0,2,1:T(8,128)(2,1)S(1)} async-done(((bf16[128,24,128]{0,2,1:T(8,128)(2,1)}), bf16[128,24,128]{0,2,1:T(8,128)(2,1)S(1)}, u32[]{:S(2)}, u32[]{:S(2)}) %all-to-all-start.3) | async-done | bytes 786464 | tf_op jit(solution)/shard_map/all_to_all | solution.py:61
  109.0 4.3 %all-to-all-start = ((bf16[128,24,128]{0,2,1:T(8,128)(2,1)}), bf16[128,24,128]{0,2,1:T(8,128)(2,1)}, u32[]{:S(2)}, u32[]{:S(2)}) async-start(bf16[128,24,128]{0,2,1:T(8,128)(2,1)} %bitcast), calls=%async_computation | async-start | bytes 1572864 | tf_op jit(solution)/shard_map/all_to_all | solution.py:54
  115.3 29.6 %all-to-all-done = bf16[128,24,128]{0,2,1:T(8,128)(2,1)} async-done(((bf16[128,24,128]{0,2,1:T(8,128)(2,1)}), bf16[128,24,128]{0,2,1:T(8,128)(2,1)}, u32[]{:S(2)}, u32[]{:S(2)}) %all-to-all-start) | async-done | bytes 786464 | tf_op jit(solution)/shard_map/all_to_all | solution.py:54
  146.4 71.2 %while.15 = (s32[]{:T(128)}, f32[384,2,128]{0,2,1:T(8,128)S(1)}, f32[384,2,128]{0,2,1:T(8,128)}, bf16[3,512,2,128]{3,2,1,0:T(2,128)(2,1)}, bf16[3,512,2,128]{3,1...) while((s32[]{:T(128)}, f32[384,2,128]{0,2,1:T(8,128)S(1)}, ...), condition=%wide.region_6.7_spmd.clone, body=%wide.region_0.6_spmd.clone.sunk | while | flops 1627100160 | bytes 34772704 | solution.py:84
  146.4 4.6 %fusion.119 = (f32[2,512]{1,0:T(2,128)S(1)}, f32[2,512,1536]{2,1,0:T(8,128)}) fusion(bf16[1536,2,128]{2,0,1:T(8,128)(2,1)S(1)} %get-tuple-element.273, bf16[3,512,2,128]{3,1,0,2:T(8,128)(2,1)S(1)} %get-tuple-element.269, s32[]{:T(128)} %get-tuple-element.253), kind=kOutput, calls=%fused_computation.51.clone.1 | convolution fusion | flops 407373312 | bytes 7344132 | tf_op jit(solution)/shard_map/while/body/eval_jaxpr/sub | solution.py:11
  151.0 4.6 %fusion.120 = f32[2,512,128]{2,1,0:T(8,128)} fusion(bf16[1536,2,128]{2,0,1:T(8,128)(2,1)S(1)} %get-tuple-element.274, f32[2,512,1536]{2,1,0:T(8,128)} %get-tuple-element.235, f32[2,512]{1,0:T(2,128)S(1)} %get-tuple-element.236), kind=kOutput, calls=%fused_computation.7.clone.1 | convolution fusion | flops 405798912 | bytes 7606272 | tf_op jit(solution)/shard_map/while/body/eval_jaxpr/gbl,lgd->bgd/dot_general | solution.py:24
  155.7 2.8 %fusion.118 = (f32[2,512]{1,0:T(2,128)S(1)}, f32[2,512,384]{1,2,0:T(8,128)}) fusion(bf16[384,2,128]{2,0,1:T(8,128)(2,1)} %get-tuple-element.270, bf16[3,512,2,128]{3,1,0,2:T(8,128)(2,1)S(1)} %get-tuple-element.269, s32[]{:T(128)} %get-tuple-element.253), kind=kOutput, calls=%fused_computation.50.clone.1 | convolution fusion | flops 101843328 | bytes 2035716 | tf_op jit(solution)/shard_map/while/body/eval_jaxpr/sub | solution.py:11
  158.4 2.2 fusion.121
  161.8 2.6 %fusion.123 = f32[384,2,128]{0,2,1:T(8,128)} fusion(f32[384,2,128]{0,2,1:T(8,128)} %get-tuple-element.255, bf16[1,512,2,128]{3,2,1,0:T(2,128)(2,1)S(1)} %get-tuple-element.237, pred[]{:T(512)S(6)} %compare.3, f32[2,512]{1,0:T(2,128)S(1)} %get-tuple-element.234, bf16[384,2,128]{2,0,1:T(8,128)(2,1)} %get-tuple-element.270, ...), kind=kOutput, calls=%fused_computation.16.clone.1 | convolution fusion | flops 203097472 | bytes 1511429 | tf_op jit(solution)/shard_map/while/body/eval_jaxpr/gbt,bgd->tgd/dot_general | solution.py:37
  164.4 2.9 %multiply_reduce_fusion.3 = (f32[2,512]{1,0:T(2,128)S(1)}, f32[2,512,384]{1,2,0:T(8,128)}) fusion(f32[2,512,384]{1,2,0:T(8,128)} %get-tuple-element.233, f32[2,512]{1,0:T(2,128)S(1)} %get-tuple-element.234, bf16[384,2,128]{2,0,1:T(8,128)(2,1)S(1)} %copy-done.8, bf16[1,512,2,128]{3,2,1,0:T(2,128)(2,1)S(1)} %get-tuple-element.237), kind=kOutput, calls=%fused_computation.10.clone.1 | convolution fusion | flops 101841920 | bytes 3612672 | tf_op jit(solution)/shard_map/while/body/eval_jaxpr/bgd,tgd->gbt/dot_general | solution.py:40
  167.3 2.7 %fusion.122 = f32[384,2,128]{0,2,1:T(8,128)S(1)} fusion(f32[2,512,384]{1,2,0:T(8,128)} %get-tuple-element.238, f32[2,512]{1,0:T(2,128)S(1)} %get-tuple-element.239, f32[384,2,128]{0,2,1:T(8,128)S(1)} %get-tuple-element.254, pred[]{:T(512)S(6)} %compare.3, bf16[3,512,2,128]{3,1,0,2:T(8,128)(2,1)S(1)} %get-tuple-element.269, s32[]{:T(128)} %get-tuple-element.253, ...), kind=kOutput, calls=%fused_computation.19.clone.1 | convolution fusion | flops 203982208 | bytes 3089409 | tf_op jit(solution)/shard_map/while/body/eval_jaxpr/gbt,bgd->tgd/dot_general | solution.py:44
  170.1 4.6 %fusion.119 = (f32[2,512]{1,0:T(2,128)S(1)}, f32[2,512,1536]{2,1,0:T(8,128)}) fusion(bf16[1536,2,128]{2,0,1:T(8,128)(2,1)S(1)} %get-tuple-element.273, bf16[3,512,2,128]{3,1,0,2:T(8,128)(2,1)S(1)} %get-tuple-element.269, s32[]{:T(128)} %get-tuple-element.253), kind=kOutput, calls=%fused_computation.51.clone.1 | convolution fusion | flops 407373312 | bytes 7344132 | tf_op jit(solution)/shard_map/while/body/eval_jaxpr/sub | solution.py:11
  174.7 4.6 %fusion.120 = f32[2,512,128]{2,1,0:T(8,128)} fusion(bf16[1536,2,128]{2,0,1:T(8,128)(2,1)S(1)} %get-tuple-element.274, f32[2,512,1536]{2,1,0:T(8,128)} %get-tuple-element.235, f32[2,512]{1,0:T(2,128)S(1)} %get-tuple-element.236), kind=kOutput, calls=%fused_computation.7.clone.1 | convolution fusion | flops 405798912 | bytes 7606272 | tf_op jit(solution)/shard_map/while/body/eval_jaxpr/gbl,lgd->bgd/dot_general | solution.py:24
  179.3 2.8 %fusion.118 = (f32[2,512]{1,0:T(2,128)S(1)}, f32[2,512,384]{1,2,0:T(8,128)}) fusion(bf16[384,2,128]{2,0,1:T(8,128)(2,1)} %get-tuple-element.270, bf16[3,512,2,128]{3,1,0,2:T(8,128)(2,1)S(1)} %get-tuple-element.269, s32[]{:T(128)} %get-tuple-element.253), kind=kOutput, calls=%fused_computation.50.clone.1 | convolution fusion | flops 101843328 | bytes 2035716 | tf_op jit(solution)/shard_map/while/body/eval_jaxpr/sub | solution.py:11
  182.0 2.2 fusion.121
  185.4 2.8 %fusion.123 = f32[384,2,128]{0,2,1:T(8,128)} fusion(f32[384,2,128]{0,2,1:T(8,128)} %get-tuple-element.255, bf16[1,512,2,128]{3,2,1,0:T(2,128)(2,1)S(1)} %get-tuple-element.237, pred[]{:T(512)S(6)} %compare.3, f32[2,512]{1,0:T(2,128)S(1)} %get-tuple-element.234, bf16[384,2,128]{2,0,1:T(8,128)(2,1)} %get-tuple-element.270, ...), kind=kOutput, calls=%fused_computation.16.clone.1 | convolution fusion | flops 203097472 | bytes 1511429 | tf_op jit(solution)/shard_map/while/body/eval_jaxpr/gbt,bgd->tgd/dot_general | solution.py:37
  188.2 2.9 %multiply_reduce_fusion.3 = (f32[2,512]{1,0:T(2,128)S(1)}, f32[2,512,384]{1,2,0:T(8,128)}) fusion(f32[2,512,384]{1,2,0:T(8,128)} %get-tuple-element.233, f32[2,512]{1,0:T(2,128)S(1)} %get-tuple-element.234, bf16[384,2,128]{2,0,1:T(8,128)(2,1)S(1)} %copy-done.8, bf16[1,512,2,128]{3,2,1,0:T(2,128)(2,1)S(1)} %get-tuple-element.237), kind=kOutput, calls=%fused_computation.10.clone.1 | convolution fusion | flops 101841920 | bytes 3612672 | tf_op jit(solution)/shard_map/while/body/eval_jaxpr/bgd,tgd->gbt/dot_general | solution.py:40
  191.1 2.7 %fusion.122 = f32[384,2,128]{0,2,1:T(8,128)S(1)} fusion(f32[2,512,384]{1,2,0:T(8,128)} %get-tuple-element.238, f32[2,512]{1,0:T(2,128)S(1)} %get-tuple-element.239, f32[384,2,128]{0,2,1:T(8,128)S(1)} %get-tuple-element.254, pred[]{:T(512)S(6)} %compare.3, bf16[3,512,2,128]{3,1,0,2:T(8,128)(2,1)S(1)} %get-tuple-element.269, s32[]{:T(128)} %get-tuple-element.253, ...), kind=kOutput, calls=%fused_computation.19.clone.1 | convolution fusion | flops 203982208 | bytes 3089409 | tf_op jit(solution)/shard_map/while/body/eval_jaxpr/gbt,bgd->tgd/dot_general | solution.py:44
  193.9 4.6 %fusion.119 = (f32[2,512]{1,0:T(2,128)S(1)}, f32[2,512,1536]{2,1,0:T(8,128)}) fusion(bf16[1536,2,128]{2,0,1:T(8,128)(2,1)S(1)} %get-tuple-element.273, bf16[3,512,2,128]{3,1,0,2:T(8,128)(2,1)S(1)} %get-tuple-element.269, s32[]{:T(128)} %get-tuple-element.253), kind=kOutput, calls=%fused_computation.51.clone.1 | convolution fusion | flops 407373312 | bytes 7344132 | tf_op jit(solution)/shard_map/while/body/eval_jaxpr/sub | solution.py:11
  198.5 4.6 %fusion.120 = f32[2,512,128]{2,1,0:T(8,128)} fusion(bf16[1536,2,128]{2,0,1:T(8,128)(2,1)S(1)} %get-tuple-element.274, f32[2,512,1536]{2,1,0:T(8,128)} %get-tuple-element.235, f32[2,512]{1,0:T(2,128)S(1)} %get-tuple-element.236), kind=kOutput, calls=%fused_computation.7.clone.1 | convolution fusion | flops 405798912 | bytes 7606272 | tf_op jit(solution)/shard_map/while/body/eval_jaxpr/gbl,lgd->bgd/dot_general | solution.py:24
  203.1 2.8 %fusion.118 = (f32[2,512]{1,0:T(2,128)S(1)}, f32[2,512,384]{1,2,0:T(8,128)}) fusion(bf16[384,2,128]{2,0,1:T(8,128)(2,1)} %get-tuple-element.270, bf16[3,512,2,128]{3,1,0,2:T(8,128)(2,1)S(1)} %get-tuple-element.269, s32[]{:T(128)} %get-tuple-element.253), kind=kOutput, calls=%fused_computation.50.clone.1 | convolution fusion | flops 101843328 | bytes 2035716 | tf_op jit(solution)/shard_map/while/body/eval_jaxpr/sub | solution.py:11
  205.8 2.2 fusion.121
  209.2 2.8 %fusion.123 = f32[384,2,128]{0,2,1:T(8,128)} fusion(f32[384,2,128]{0,2,1:T(8,128)} %get-tuple-element.255, bf16[1,512,2,128]{3,2,1,0:T(2,128)(2,1)S(1)} %get-tuple-element.237, pred[]{:T(512)S(6)} %compare.3, f32[2,512]{1,0:T(2,128)S(1)} %get-tuple-element.234, bf16[384,2,128]{2,0,1:T(8,128)(2,1)} %get-tuple-element.270, ...), kind=kOutput, calls=%fused_computation.16.clone.1 | convolution fusion | flops 203097472 | bytes 1511429 | tf_op jit(solution)/shard_map/while/body/eval_jaxpr/gbt,bgd->tgd/dot_general | solution.py:37
  211.9 2.9 %multiply_reduce_fusion.3 = (f32[2,512]{1,0:T(2,128)S(1)}, f32[2,512,384]{1,2,0:T(8,128)}) fusion(f32[2,512,384]{1,2,0:T(8,128)} %get-tuple-element.233, f32[2,512]{1,0:T(2,128)S(1)} %get-tuple-element.234, bf16[384,2,128]{2,0,1:T(8,128)(2,1)S(1)} %copy-done.8, bf16[1,512,2,128]{3,2,1,0:T(2,128)(2,1)S(1)} %get-tuple-element.237), kind=kOutput, calls=%fused_computation.10.clone.1 | convolution fusion | flops 101841920 | bytes 3612672 | tf_op jit(solution)/shard_map/while/body/eval_jaxpr/bgd,tgd->gbt/dot_general | solution.py:40
  214.9 2.7 %fusion.122 = f32[384,2,128]{0,2,1:T(8,128)S(1)} fusion(f32[2,512,384]{1,2,0:T(8,128)} %get-tuple-element.238, f32[2,512]{1,0:T(2,128)S(1)} %get-tuple-element.239, f32[384,2,128]{0,2,1:T(8,128)S(1)} %get-tuple-element.254, pred[]{:T(512)S(6)} %compare.3, bf16[3,512,2,128]{3,1,0,2:T(8,128)(2,1)S(1)} %get-tuple-element.269, s32[]{:T(128)} %get-tuple-element.253, ...), kind=kOutput, calls=%fused_computation.19.clone.1 | convolution fusion | flops 203982208 | bytes 3089409 | tf_op jit(solution)/shard_map/while/body/eval_jaxpr/gbt,bgd->tgd/dot_general | solution.py:44
  219.9 3.6 %all-to-all-start.4 = ((bf16[384,2,256]{2,1,0:T(2,128)(2,1)}), bf16[384,2,256]{2,1,0:T(2,128)(2,1)S(1)}, u32[]{:S(2)}, u32[]{:S(2)}) async-start(bf16[384,2,256]{2,1,0:T(2,128)(2,1)} %copy.81), calls=%async_computation.4 | async-start | bytes 786432 | tf_op jit(solution)/shard_map/all_to_all | solution.py:93
  224.9 18.3 %all-to-all-done.4 = bf16[384,2,256]{2,1,0:T(2,128)(2,1)S(1)} async-done(((bf16[384,2,256]{2,1,0:T(2,128)(2,1)}), bf16[384,2,256]{2,1,0:T(2,128)(2,1)S(1)}, u32[]{:S(2)}, u32[]{:S(2)}) %all-to-all-start.4) | async-done | bytes 393248 | tf_op jit(solution)/shard_map/all_to_all | solution.py:93
  (54 shorter events, 17.5 us)
Async XLA Ops:
  0.6 17.2 %copy-start = (bf16[1,128,3072]{2,1,0:T(8,128)(2,1)S(1)}, bf16[1,128,3072]{2,1,0:T(8,128)(2,1)}, u32[]{:S(2)}) copy-start(bf16[1,128,3072]{2,1,0:T(8,128)(2,1)} %param.8) | copy-start | bytes 2359300
  2.6 34.9 %all-to-all-start.1 = ((bf16[32,24,256]{2,0,1:T(8,128)(2,1)}), bf16[32,24,256]{2,0,1:T(8,128)(2,1)S(1)}, u32[]{:S(2)}, u32[]{:S(2)}) async-start(bf16[32,24,256]{2,0,1:T(8,128)(2,1)} %copy.70), calls=%async_computation.1 | async-start | bytes 786432 | tf_op jit(solution)/shard_map/all_to_all | solution.py:58
  17.8 23.4 %copy-start.1 = (bf16[1,128,3072]{2,1,0:T(8,128)(2,1)S(1)}, bf16[1,128,3072]{2,1,0:T(8,128)(2,1)}, u32[]{:S(2)}) copy-start(bf16[1,128,3072]{2,1,0:T(8,128)(2,1)} %param.9) | copy-start | bytes 2359300
  37.5 35.9 %all-to-all-start.2 = ((bf16[128,24,128]{0,2,1:T(8,128)(2,1)}), bf16[128,24,128]{0,2,1:T(8,128)(2,1)S(1)}, u32[]{:S(2)}, u32[]{:S(2)}) async-start(bf16[128,24,128]{0,2,1:T(8,128)(2,1)} %bitcast.8), calls=%async_computation.2 | async-start | bytes 1572864 | tf_op jit(solution)/shard_map/all_to_all | solution.py:60
  41.2 35.9 %copy-start.2 = (bf16[1,128,3072]{2,1,0:T(8,128)(2,1)S(1)}, bf16[1,128,3072]{2,1,0:T(8,128)(2,1)}, u32[]{:S(2)}) copy-start(bf16[1,128,3072]{2,1,0:T(8,128)(2,1)} %param.7) | copy-start | bytes 2359300
  73.5 35.5 %all-to-all-start.3 = ((bf16[128,24,128]{0,2,1:T(8,128)(2,1)}), bf16[128,24,128]{0,2,1:T(8,128)(2,1)S(1)}, u32[]{:S(2)}, u32[]{:S(2)}) async-start(bf16[128,24,128]{0,2,1:T(8,128)(2,1)} %bitcast.13), calls=%async_computation.3 | async-start | bytes 1572864 | tf_op jit(solution)/shard_map/all_to_all | solution.py:61
  77.2 36.2 %copy-start.3 = (bf16[1,1536,256]{2,1,0:T(8,128)(2,1)S(1)}, bf16[1,1536,256]{2,1,0:T(8,128)(2,1)}, u32[]{:S(2)}) copy-start(bf16[1,1536,256]{2,1,0:T(8,128)(2,1)} %param.11) | copy-start | bytes 2359300
  109.0 35.9 %all-to-all-start = ((bf16[128,24,128]{0,2,1:T(8,128)(2,1)}), bf16[128,24,128]{0,2,1:T(8,128)(2,1)}, u32[]{:S(2)}, u32[]{:S(2)}) async-start(bf16[128,24,128]{0,2,1:T(8,128)(2,1)} %bitcast), calls=%async_computation | async-start | bytes 1572864 | tf_op jit(solution)/shard_map/all_to_all | solution.py:54
  115.3 31.1 %copy-start.7 = (f32[384,2,128]{0,2,1:T(8,128)S(1)}, f32[384,2,128]{0,2,1:T(8,128)}, u32[]{:S(2)}) copy-start(f32[384,2,128]{0,2,1:T(8,128)} %custom-call) | copy-start | bytes 1179652
  146.4 4.6 %copy-start.4 = (bf16[1536,2,128]{2,0,1:T(8,128)(2,1)}, bf16[1536,2,128]{2,0,1:T(8,128)(2,1)S(1)}, u32[]{:S(2)}) copy-start(bf16[1536,2,128]{2,0,1:T(8,128)(2,1)S(1)} %get-tuple-element.274) | copy-start | bytes 2359300 | tf_op jit(solution)/shard_map/while
  155.7 2.8 %copy-start.8 = (bf16[384,2,128]{2,0,1:T(8,128)(2,1)S(1)}, bf16[384,2,128]{2,0,1:T(8,128)(2,1)}, u32[]{:S(2)}) copy-start(bf16[384,2,128]{2,0,1:T(8,128)(2,1)} %get-tuple-element.272) | copy-start | bytes 589828 | tf_op jit(solution)/shard_map/while
  167.3 2.7 %copy-start.5 = (bf16[1536,2,128]{2,0,1:T(8,128)(2,1)S(1)}, bf16[1536,2,128]{2,0,1:T(8,128)(2,1)}, u32[]{:S(2)}) copy-start(bf16[1536,2,128]{2,0,1:T(8,128)(2,1)} %copy-done.4) | copy-start | bytes 2359300 | tf_op jit(solution)/shard_map/while
  170.1 4.6 %copy-start.4 = (bf16[1536,2,128]{2,0,1:T(8,128)(2,1)}, bf16[1536,2,128]{2,0,1:T(8,128)(2,1)S(1)}, u32[]{:S(2)}) copy-start(bf16[1536,2,128]{2,0,1:T(8,128)(2,1)S(1)} %get-tuple-element.274) | copy-start | bytes 2359300 | tf_op jit(solution)/shard_map/while
  179.3 2.8 %copy-start.8 = (bf16[384,2,128]{2,0,1:T(8,128)(2,1)S(1)}, bf16[384,2,128]{2,0,1:T(8,128)(2,1)}, u32[]{:S(2)}) copy-start(bf16[384,2,128]{2,0,1:T(8,128)(2,1)} %get-tuple-element.272) | copy-start | bytes 589828 | tf_op jit(solution)/shard_map/while
  191.1 2.7 %copy-start.5 = (bf16[1536,2,128]{2,0,1:T(8,128)(2,1)S(1)}, bf16[1536,2,128]{2,0,1:T(8,128)(2,1)}, u32[]{:S(2)}) copy-start(bf16[1536,2,128]{2,0,1:T(8,128)(2,1)} %copy-done.4) | copy-start | bytes 2359300 | tf_op jit(solution)/shard_map/while
  193.8 4.6 %copy-start.4 = (bf16[1536,2,128]{2,0,1:T(8,128)(2,1)}, bf16[1536,2,128]{2,0,1:T(8,128)(2,1)S(1)}, u32[]{:S(2)}) copy-start(bf16[1536,2,128]{2,0,1:T(8,128)(2,1)S(1)} %get-tuple-element.274) | copy-start | bytes 2359300 | tf_op jit(solution)/shard_map/while
  203.1 2.8 %copy-start.8 = (bf16[384,2,128]{2,0,1:T(8,128)(2,1)S(1)}, bf16[384,2,128]{2,0,1:T(8,128)(2,1)}, u32[]{:S(2)}) copy-start(bf16[384,2,128]{2,0,1:T(8,128)(2,1)} %get-tuple-element.272) | copy-start | bytes 589828 | tf_op jit(solution)/shard_map/while
  214.9 2.7 %copy-start.5 = (bf16[1536,2,128]{2,0,1:T(8,128)(2,1)S(1)}, bf16[1536,2,128]{2,0,1:T(8,128)(2,1)}, u32[]{:S(2)}) copy-start(bf16[1536,2,128]{2,0,1:T(8,128)(2,1)} %copy-done.4) | copy-start | bytes 2359300 | tf_op jit(solution)/shard_map/while
  217.6 5.9 %copy-start.6 = (bf16[3,512,2,128]{3,2,1,0:T(2,128)(2,1)S(1)}, bf16[3,512,2,128]{3,2,1,0:T(2,128)(2,1)}, u32[]{:S(2)}) copy-start(bf16[3,512,2,128]{3,2,1,0:T(2,128)(2,1)} %get-tuple-element.56) | copy-start | bytes 2359300
  219.9 23.3 %all-to-all-start.4 = ((bf16[384,2,256]{2,1,0:T(2,128)(2,1)}), bf16[384,2,256]{2,1,0:T(2,128)(2,1)S(1)}, u32[]{:S(2)}, u32[]{:S(2)}) async-start(bf16[384,2,256]{2,1,0:T(2,128)(2,1)} %copy.81), calls=%async_computation.4 | async-start | bytes 786432 | tf_op jit(solution)/shard_map/all_to_all | solution.py:93
where the time goes:
time: 246 us; the launch traced here: 245 us
  waiting for transfers between devices  128 us (52%)
  matrix products  67.5 us (27%)
  starting transfers between devices  30.4 us (12%)
  local copies, waits for them, and re-layouts  16.3 us (7%)
    all_to_all x1, waiting for transfers between devices, per_device(): lax.all_to_all(keys.reshape(shape_in), 'head', split_axis=1, concat_axis=...  31.1 us
    all_to_all x1, waiting for transfers between devices, per_device(): lax.all_to_all(values.reshape(shape_in), 'head', split_axis=1, concat_axi...  30.7 us
    all_to_all x1, waiting for transfers between devices, per_device(): lax.all_to_all(queries.reshape(shape_in), 'head', split_axis=1, concat_ax...  29.6 us
    sub x6, matrix products, softmax_rows(): weights = jnp.exp(scores - top)  22.1 us
    all_to_all x1, waiting for transfers between devices, per_device(): lax.all_to_all(text_local, 'head', split_axis=1, concat_axis=0, tiled=True)  18.6 us
    all_to_all x1, waiting for transfers between devices, per_device(): lax.all_to_all(grad_term, 'head', split_axis=0, concat_axis=1, tiled=True)  18.3 us
    all_to_all x1, starting transfers between devices, per_device(): lax.all_to_all(text_local, 'head', split_axis=1, concat_axis=0, tiled=True)  15.2 us
    dot_general x3, matrix products, self_part(): jnp.einsum('gbl,lgd->bgd', probs, value_all, preferred_element_type=jnp.f...  13.8 us
  transfers between devices with their start and end apart: 5, of which 5 were waited for; matrix products, arithmetic and copies ran while one was open for 3% of the time, Pallas kernels for 0%

commit v1 on v0

v1 whole, which is shorter than its diff:
```python
import functools
import math

import jax
import jax.numpy as jnp
from jax import lax
from jax.experimental import pallas as pl
from jax.experimental.pallas import tpu as pltpu
from jax.sharding import PartitionSpec as P

HD = 128
MESH = pl.DeviceIdType.MESH
BF16 = jnp.bfloat16
F32 = jnp.float32


def dot(a, b, ca, cb):
    return lax.dot_general(a, b, (((ca,), (cb,)), ((), ())), preferred_element_type=F32)


def near_first(n):
    order = []
    for d in range(1, n // 2 + 1):
        order.append(d)
        if n - d != d:
            order.append(n - d)
    return order


def kernel(
    n, q_in, k_in, v_in, t_in, g_in, att_out, tg_out,
    q_buf, k_buf, v_buf, t_buf, g_buf, p_buf, cross_buf, att_buf, dk_acc, dv_acc, tg_buf,
    send_sem, recv_sem, local_sem, out_sem, gsend_sem, grecv_sem,
):
    me = lax.axis_index("head")
    rows = q_in.shape[0]
    trows = t_in.shape[0]
    width = q_buf.shape[1]
    twidth = t_buf.shape[1]
    length = q_buf.shape[0]
    groups = width // HD
    factor = HD ** -0.5 * math.log2(math.e)

    own = []
    for a, (src, dst, h, w) in enumerate(
        ((t_in, t_buf, trows, twidth), (q_in, q_buf, rows, width), (k_in, k_buf, rows, width), (v_in, v_buf, rows, width))
    ):
        copy = pltpu.make_async_copy(
            src.at[:, pl.ds(pl.multiple_of(me * w, w), w)],
            dst.at[pl.ds(pl.multiple_of(me * h, h), h), :],
            local_sem.at[a],
        )
        copy.start()
        own.append(copy)
    g_copy = pltpu.make_async_copy(g_in, g_buf, local_sem.at[4])
    g_copy.start()

    barrier = pltpu.get_barrier_semaphore()
    for d in range(1, n):
        pl.semaphore_signal(barrier, inc=1, device_id={"head": lax.rem(me + d, n)}, device_id_type=MESH)
    pl.semaphore_wait(barrier, n - 1)

    sends = [[], [], [], []]
    for a, (src, dst, h, w) in enumerate(
        ((t_in, t_buf, trows, twidth), (q_in, q_buf, rows, width), (k_in, k_buf, rows, width), (v_in, v_buf, rows, width))
    ):
        for d in near_first(n):
            to = lax.rem(me + d, n)
            copy = pltpu.make_async_remote_copy(
                src_ref=src.at[:, pl.ds(pl.multiple_of(to * w, w), w)],
                dst_ref=dst.at[pl.ds(pl.multiple_of(me * h, h), h), :],
                send_sem=send_sem.at[a, d],
                recv_sem=recv_sem.at[a, d],
                device_id={"head": to},
                device_id_type=MESH,
            )
            copy.start()
            sends[a].append(copy)

    def arrive(a):
        own[a].wait()
        for copy in sends[a]:
            copy.wait_recv()

    g_copy.wait()
    arrive(0)
    arrive(1)

    dk_acc[...] = jnp.zeros_like(dk_acc)
    dv_acc[...] = jnp.zeros_like(dv_acc)
    cross_rows = 256

    def cross_step(i, carry):
        at = pl.ds(pl.multiple_of(i * cross_rows, cross_rows), cross_rows)
        for h in range(groups):
            cols = pl.ds(h * HD, HD)
            q = q_buf[at, cols]
            g = g_buf[at, cols]
            kt = t_buf[:, pl.ds(2 * h * HD, HD)]
            vt = t_buf[:, pl.ds((2 * h + 1) * HD, HD)]
            x = dot(kt, q, 1, 1)
            e = jnp.exp2((x - jnp.max(x, axis=0, keepdims=True)) * factor)
            r = e * (1.0 / jnp.sum(e, axis=0, keepdims=True))
            rb = r.astype(BF16)
            dr = dot(vt, g, 1, 1)
            dx = (r * (dr - jnp.sum(dr * r, axis=0, keepdims=True))).astype(BF16)
            dk_acc[h] += dot(dx, q, 1, 0)
            dv_acc[h] += dot(rb, g, 1, 0)
            cross_buf[at, cols] = dot(rb, vt, 0, 0)
        return carry

    lax.fori_loop(0, length // cross_rows, cross_step, 0)
    for h in range(groups):
        tg_buf[:, pl.ds(2 * h * HD, HD)] = (dk_acc[h] * (HD ** -0.5)).astype(BF16)
        tg_buf[:, pl.ds((2 * h + 1) * HD, HD)] = dv_acc[h].astype(BF16)
    own_grad = pltpu.make_async_copy(
        tg_buf.at[pl.ds(pl.multiple_of(me * trows, trows), trows), :],
        tg_out.at[:, pl.ds(pl.multiple_of(me * twidth, twidth), twidth)],
        local_sem.at[5],
    )
    own_grad.start()
    returns = []
    for d in near_first(n):
        to = lax.rem(me + d, n)
        copy = pltpu.make_async_remote_copy(
            src_ref=tg_buf.at[pl.ds(pl.multiple_of(to * trows, trows), trows), :],
            dst_ref=tg_out.at[:, pl.ds(pl.multiple_of(me * twidth, twidth), twidth)],
            send_sem=gsend_sem.at[d],
            recv_sem=grecv_sem.at[d],
            device_id={"head": to},
            device_id_type=MESH,
        )
        copy.start()
        returns.append(copy)

    arrive(2)
    block = 256

    def score_step(i, carry):
        at = pl.ds(pl.multiple_of(i * block, block), block)
        for h in range(groups):
            cols = pl.ds(h * HD, HD)
            s = dot(q_buf[at, cols], k_buf[:, cols], 1, 1)
            top = jnp.max(s, axis=1, keepdims=True)
            p_buf[h, at, :] = jnp.exp2((s - top) * factor).astype(BF16)
        return carry

    lax.fori_loop(0, length // block, score_step, 0)

    arrive(3)

    def out_copy(i):
        at = pl.ds(pl.multiple_of(i * block, block), block)
        return pltpu.make_async_copy(att_buf.at[at, :], att_out.at[at, :], out_sem.at[i])

    def value_step(i, carry):
        at = pl.ds(pl.multiple_of(i * block, block), block)
        for h in range(groups):
            cols = pl.ds(h * HD, HD)
            v = v_buf[:, cols]
            both = dot(p_buf[h, at, :], jnp.concatenate([v, jnp.ones_like(v)], axis=1), 1, 0)
            att_buf[at, cols] = (both[:, :HD] / both[:, HD:] + cross_buf[at, cols]).astype(BF16)
        out_copy(i).start()
        return carry

    lax.fori_loop(0, length // block, value_step, 0)

    for a in range(4):
        for copy in sends[a]:
            copy.wait_send()
    own_grad.wait()
    for copy in returns:
        copy.wait()
    for i in range(length // block):
        out_copy(i).wait()


def per_device(n, queries, keys, values, text_kv, cotangent):
    rows, columns = queries.shape[1:]
    trows, tcolumns = text_kv.shape[1:]
    length, width = cotangent.shape[1:]
    twidth = tcolumns // n
    text = trows * n
    groups = width // HD
    attended, grad = pl.pallas_call(
        functools.partial(kernel, n),
        out_shape=(
            jax.ShapeDtypeStruct((length, width), BF16),
            jax.ShapeDtypeStruct((trows, tcolumns), BF16),
        ),
        in_specs=[pl.BlockSpec(memory_space=pl.ANY)] * 5,
        out_specs=(pl.BlockSpec(memory_space=pl.ANY),) * 2,
        scratch_shapes=[
            pltpu.VMEM((length, width), BF16),
            pltpu.VMEM((length, width), BF16),
            pltpu.VMEM((length, width), BF16),
            pltpu.VMEM((text, twidth), BF16),
            pltpu.VMEM((length, width), BF16),
            pltpu.VMEM((groups, length, length), BF16),
            pltpu.VMEM((length, width), F32),
            pltpu.VMEM((length, width), BF16),
            pltpu.VMEM((groups, text, HD), F32),
            pltpu.VMEM((groups, text, HD), F32),
            pltpu.VMEM((text, twidth), BF16),
            pltpu.SemaphoreType.DMA((4, n)),
            pltpu.SemaphoreType.DMA((4, n)),
            pltpu.SemaphoreType.DMA((6,)),
            pltpu.SemaphoreType.DMA((length // 256,)),
            pltpu.SemaphoreType.DMA((n,)),
            pltpu.SemaphoreType.DMA((n,)),
        ],
        compiler_params=pltpu.CompilerParams(
            collective_id=0, has_side_effects=True, vmem_limit_bytes=60 * 2**20
        ),
    )(queries[0], keys[0], values[0], text_kv[0], cotangent[0])
    return attended[None], grad[None]


def solution(mesh):
    split = P(("seq", "rep"), "head", None)
    kept = P(("seq", "rep"), None, "head")
    return jax.shard_map(
        functools.partial(per_device, mesh.shape["head"]),
        mesh=mesh,
        in_specs=(split, split, split, split, kept),
        out_specs=(kept, split),
        check_vma=False,
    )
```

time: 246 us -> 124 us (0.50)
  waiting for transfers between devices: 128 us -> 0 us
  Pallas kernels: 0 us -> 120 us
  matrix products: 67.5 us -> 0 us
  starting transfers between devices: 30.4 us -> 0 us
  local copies, waits for them, and re-layouts: 16.3 us -> 2.86 us
    all_to_all x5 -> x0, waiting for transfers between devices: 128 us -> none  [the longest x1 31.1 us: per_device(): lax.all_to_all(keys.reshape(shape_in), 'head', split_axis=1, concat_axis=...]
    pallas_call x0 -> x1, Pallas kernels: none -> 120 us  [per_device(): pl.pallas_call(functools.partial(kernel, n), out_shape=(jax.ShapeDtypeStr...]
    dot_general x15 -> x0, matrix products: 45.4 us -> none  [the longest x3 13.8 us: self_part(): jnp.einsum('gbl,lgd->bgd', probs, value_all, preferred_element_type=jnp.f...]
    all_to_all x5 -> x0, starting transfers between devices: 30.4 us -> none  [the longest x1 15.2 us: per_device(): lax.all_to_all(text_local, 'head', split_axis=1, concat_axis=0, tiled=True)]
    sub x6 -> x0, matrix products: 22.1 us -> none  [softmax_rows(): weights = jnp.exp(scores - top)]
    dynamic_update_slice x3 -> x0, local copies, waits for them, and re-layouts: 3.48 us -> none  [per_device(): lax.scan(both_step, (zeros, zeros), (query_blocks, grad_blocks))]
    reshape x4 -> x0, local copies, waits for them, and re-layouts: 3.42 us -> none  [the longest x1 1.38 us: per_device(): attended = outputs.reshape(1, length, groups * HD)]
    all_to_all x6 -> x0, local copies, waits for them, and re-layouts: 2.74 us -> none  [the longest x1 1.5 us: per_device(): lax.all_to_all(queries.reshape(shape_in), 'head', split_axis=1, concat_ax...]
  transfers between devices with their start and end apart: 5 -> 0, of which waited for: 5 -> 0; matrix products, arithmetic and copies ran while one was open for 3% -> 0% of each run, Pallas kernels for 0% -> 0%
where the time goes in v1:
time: 124 us
  Pallas kernels  120 us (97%)
  local copies, waits for them, and re-layouts  2.86 us (2%)
    pallas_call x1, Pallas kernels, per_device(): pl.pallas_call(functools.partial(kernel, n), out_shape=(jax.ShapeDtypeStr...  120 us
    unnamed x4, local copies, waits for them, and re-layouts  2.86 us

profile of v1, /device:TPU:56, one launch (start us, length us, event | category | flops | bytes accessed | tf_op | source)
XLA Modules:
  0.0 123.6 jit_solution(8753486794507874017)
XLA Ops:
  0.6 120.1 %shard_map.68 = (bf16[1536,256]{1,0:T(8,128)(2,1)}, bf16[32,6144]{1,0:T(8,128)(2,1)}) custom-call(bf16[128,3072]{1,0:T(8,128)(2,1)} %bitcast.7, bf16[128,3072]{1,0:T(8,128)(2,1)} %bitcast.8, bf16[128,3072]{1,0:T(8,128)(2,1)} %bitcast.9, bf16[32,6144]{1,0:T(8,128)(2,1)} %bitcast.12, bf16[1536,256]{1,0:T(8,128)(2,1)} %bitcast.10), custom_call_target="tpu_custom_call" | custom-call | tf_op jit(solution)/shard_map/pallas_call | solution.py:185
  120.7 0.0 copy-start
  120.7 2.1 %copy.9 = bf16[1,1536,256]{2,1,0:T(8,128)(2,1)} copy(bf16[1,1536,256]{2,1,0:T(8,128)(2,1)} %bitcast.11) | data formatting | bytes 1572864
  122.8 0.0 copy-done
  122.8 0.7 copy.10
Async XLA Ops:
  120.7 2.1 %copy-start = (bf16[32,6144]{1,0:T(8,128)(2,1)S(1)}, bf16[32,6144]{1,0:T(8,128)(2,1)}, u32[]{:S(2)}) copy-start(bf16[32,6144]{1,0:T(8,128)(2,1)} %get-tuple-element.5) | copy-start | bytes 1179652

commit v2 on v1

--- a/solution.py
+++ b/solution.py
@@ -18,19 +18,35 @@
     return lax.dot_general(a, b, (((ca,), (cb,)), ((), ())), preferred_element_type=F32)
 
 
-def near_first(n):
+def near_first(n, at):
     order = []
     for d in range(1, n // 2 + 1):
-        order.append(d)
+        order.append((at + d) % n)
         if n - d != d:
-            order.append(n - d)
+            order.append((at - d) % n)
     return order
+
+
+def below_first(n, at):
+    return [to for to in near_first(n, at) if to < at] + list(range(at + 1, n))
+
+
+def pick(me, column):
+    value = jnp.int32(column[0])
+    for at in range(1, len(column)):
+        value = jnp.where(me == at, jnp.int32(column[at]), value)
+    return value
+
+
+def peers(n, me, order):
+    table = [order(n, at) for at in range(n)]
+    return [pick(me, [row[j] for row in table]) for j in range(n - 1)]
 
 
 def kernel(
     n, q_in, k_in, v_in, t_in, g_in, att_out, tg_out,
     q_buf, k_buf, v_buf, t_buf, g_buf, p_buf, cross_buf, att_buf, dk_acc, dv_acc, tg_buf,
-    send_sem, recv_sem, local_sem, out_sem, gsend_sem, grecv_sem,
+    send_sem, recv_sem, local_sem, out_sem, gsend_sem, grecv_sem, in_sem,
 ):
     me = lax.axis_index("head")
     rows = q_in.shape[0]
@@ -56,31 +72,53 @@
     g_copy.start()
 
     barrier = pltpu.get_barrier_semaphore()
-    for d in range(1, n):
-        pl.semaphore_signal(barrier, inc=1, device_id={"head": lax.rem(me + d, n)}, device_id_type=MESH)
-    pl.semaphore_wait(barrier, n - 1)
-
-    sends = [[], [], [], []]
-    for a, (src, dst, h, w) in enumerate(
-        ((t_in, t_buf, trows, twidth), (q_in, q_buf, rows, width), (k_in, k_buf, rows, width), (v_in, v_buf, rows, width))
-    ):
-        for d in near_first(n):
-            to = lax.rem(me + d, n)
-            copy = pltpu.make_async_remote_copy(
-                src_ref=src.at[:, pl.ds(pl.multiple_of(to * w, w), w)],
-                dst_ref=dst.at[pl.ds(pl.multiple_of(me * h, h), h), :],
-                send_sem=send_sem.at[a, d],
-                recv_sem=recv_sem.at[a, d],
-                device_id={"head": to},
-                device_id_type=MESH,
-            )
-            copy.start()
-            sends[a].append(copy)
+
+    @pl.when(me > 0)
+    def _():
+        pl.semaphore_wait(barrier, 1)
+
+    @pl.when(me < n - 1)
+    def _():
+        pl.semaphore_signal(barrier, inc=1, device_id={"head": lax.rem(me + 1, n)}, device_id_type=MESH)
+
+    for w in range(n - 1):
+
+        @pl.when(w < me)
+        def _(w=w):
+            pl.semaphore_signal(in_sem.at[me], inc=1, device_id={"head": w}, device_id_type=MESH)
+
+    arrays = ((t_in, t_buf, trows, twidth), (q_in, q_buf, rows, width), (k_in, k_buf, rows, width), (v_in, v_buf, rows, width))
+
+    def block_copy(a, source, to, sem):
+        src, dst, h, w = arrays[a]
+        return pltpu.make_async_remote_copy(
+            src_ref=src.at[:, pl.ds(pl.multiple_of(to * w, w), w)],
+            dst_ref=dst.at[pl.ds(pl.multiple_of(source * h, h), h), :],
+            send_sem=send_sem.at[a, sem],
+            recv_sem=recv_sem.at[a, source],
+            device_id={"head": to},
+            device_id_type=MESH,
+        )
+
+    for to in peers(n, me, below_first):
+
+        @pl.when(to > me)
+        def _():
+            pl.semaphore_wait(in_sem.at[to], 1)
+
+        block_copy(0, me, to, to).start()
+        block_copy(1, me, to, to).start()
+
+    for a in (2, 3):
+        for to in peers(n, me, near_first):
+            block_copy(a, me, to, to).start()
+
+    others = [lax.rem(me + d, n) for d in range(1, n)]
 
     def arrive(a):
         own[a].wait()
-        for copy in sends[a]:
-            copy.wait_recv()
+        for other in others:
+            block_copy(a, other, other, other).wait_recv()
 
     g_copy.wait()
     arrive(0)
@@ -119,19 +157,18 @@
         local_sem.at[5],
     )
     own_grad.start()
-    returns = []
-    for d in near_first(n):
-        to = lax.rem(me + d, n)
-        copy = pltpu.make_async_remote_copy(
+    def grad_copy(source, to, sem):
+        return pltpu.make_async_remote_copy(
             src_ref=tg_buf.at[pl.ds(pl.multiple_of(to * trows, trows), trows), :],
-            dst_ref=tg_out.at[:, pl.ds(pl.multiple_of(me * twidth, twidth), twidth)],
-            send_sem=gsend_sem.at[d],
-            recv_sem=grecv_sem.at[d],
+            dst_ref=tg_out.at[:, pl.ds(pl.multiple_of(source * twidth, twidth), twidth)],
+            send_sem=gsend_sem.at[sem],
+            recv_sem=grecv_sem.at[source],
             device_id={"head": to},
             device_id_type=MESH,
         )
-        copy.start()
-        returns.append(copy)
+
+    for to in peers(n, me, near_first):
+        grad_copy(me, to, to).start()
 
     arrive(2)
     block = 256
@@ -165,14 +202,25 @@
 
     lax.fori_loop(0, length // block, value_step, 0)
 
-    for a in range(4):
-        for copy in sends[a]:
-            copy.wait_send()
     own_grad.wait()
-    for copy in returns:
-        copy.wait()
+    for other in others:
+        for a in range(4):
+            block_copy(a, me, other, other).wait_send()
+        grad_copy(me, other, other).wait_send()
+        grad_copy(other, other, other).wait_recv()
     for i in range(length // block):
         out_copy(i).wait()
+
+
+def place(a_in, b_in, a_out, b_out, sems):
+    copies = [
+        pltpu.make_async_copy(a_in, a_out, sems.at[0]),
+        pltpu.make_async_copy(b_in, b_out, sems.at[1]),
+    ]
+    for copy in copies:
+        copy.start()
+    for copy in copies:
+        copy.wait()
 
 
 def per_device(n, queries, keys, values, text_kv, cotangent):
@@ -185,8 +233,8 @@
     attended, grad = pl.pallas_call(
         functools.partial(kernel, n),
         out_shape=(
-            jax.ShapeDtypeStruct((length, width), BF16),
-            jax.ShapeDtypeStruct((trows, tcolumns), BF16),
+            pltpu.VMEM((length, width), BF16),
+            pltpu.VMEM((trows, tcolumns), BF16),
         ),
         in_specs=[pl.BlockSpec(memory_space=pl.ANY)] * 5,
         out_specs=(pl.BlockSpec(memory_space=pl.ANY),) * 2,
@@ -208,11 +256,22 @@
             pltpu.SemaphoreType.DMA((length // 256,)),
             pltpu.SemaphoreType.DMA((n,)),
             pltpu.SemaphoreType.DMA((n,)),
+            pltpu.SemaphoreType.REGULAR((n,)),
         ],
         compiler_params=pltpu.CompilerParams(
-            collective_id=0, has_side_effects=True, vmem_limit_bytes=60 * 2**20
+            collective_id=0, has_side_effects=True, vmem_limit_bytes=40 * 2**20
         ),
-    )(queries[0], keys[0], values[0], text_kv[0], cotangent[0])
+    )(*(pltpu.with_memory_space_constraint(x[0], pltpu.HBM) for x in (queries, keys, values, text_kv, cotangent)))
+    attended, grad = pl.pallas_call(
+        place,
+        out_shape=(
+            jax.ShapeDtypeStruct((length, width), BF16),
+            jax.ShapeDtypeStruct((trows, tcolumns), BF16),
+        ),
+        in_specs=[pl.BlockSpec(memory_space=pl.ANY)] * 2,
+        out_specs=(pl.BlockSpec(memory_space=pltpu.HBM),) * 2,
+        scratch_shapes=[pltpu.SemaphoreType.DMA((2,))],
+    )(*(pltpu.with_memory_space_constraint(x, pltpu.VMEM) for x in (attended, grad)))
     return attended[None], grad[None]
 
 

time: 124 us -> 119 us (0.960)
  local copies, waits for them, and re-layouts: 2.86 us -> 0 us
  Pallas kernels: 120 us -> 118 us
    unnamed x4 -> x0, local copies, waits for them, and re-layouts: 2.86 us -> none
    pallas_call x1 -> x2, Pallas kernels: 120 us -> 118 us  [the longest x1 117 us: per_device(): pl.pallas_call(functools.partial(kernel, n), out_shape=(pltpu.VMEM((lengt...]
where the time goes in v2:
time: 119 us
  Pallas kernels  118 us (99%)
    pallas_call x1, Pallas kernels, per_device(): pl.pallas_call(functools.partial(kernel, n), out_shape=(pltpu.VMEM((lengt...  117 us

profile of v2, /device:TPU:56, one launch (start us, length us, event | category | flops | bytes accessed | tf_op | source)
XLA Modules:
  0.0 119.0 jit_solution(12288902422233342492)
XLA Ops:
  0.6 117.3 %shard_map.68 = (bf16[1536,256]{1,0:T(8,128)(2,1)S(1)}, bf16[32,6144]{1,0:T(8,128)(2,1)S(1)}) custom-call(bf16[128,3072]{1,0:T(8,128)(2,1)} %bitcast.7, bf16[128,3072]{1,0:T(8,128)(2,1)} %bitcast.8, bf16[128,3072]{1,0:T(8,128)(2,1)} %bitcast.9, bf16[32,6144]{1,0:T(8,128)(2,1)} %bitcast.11, bf16[1536,256]{1,0:T(8,128)(2,1)} %bitcast.10), custom_call_target="tpu_custom_call" | custom-call | tf_op jit(solution)/shard_map/pallas_call | solution.py:233
  118.0 1.0 shard_map.69

commit v3 on v2

--- a/solution.py
+++ b/solution.py
@@ -31,6 +31,10 @@
     return [to for to in near_first(n, at) if to < at] + list(range(at + 1, n))
 
 
+def ascending(n, at):
+    return [to for to in range(n) if to != at]
+
+
 def pick(me, column):
     value = jnp.int32(column[0])
     for at in range(1, len(column)):
@@ -45,8 +49,8 @@
 
 def kernel(
     n, q_in, k_in, v_in, t_in, g_in, att_out, tg_out,
-    q_buf, k_buf, v_buf, t_buf, g_buf, p_buf, cross_buf, att_buf, dk_acc, dv_acc, tg_buf,
-    send_sem, recv_sem, local_sem, out_sem, gsend_sem, grecv_sem, in_sem,
+    q_buf, k_buf, v_buf, t_buf, g_buf, p_buf, cross_buf, att_buf, dk_acc, dv_acc, tg_buf, relay_buf,
+    send_sem, recv_sem, local_sem, out_sem, gsend_sem, grecv_sem, in_sem, relay_sem, pass_sem,
 ):
     me = lax.axis_index("head")
     rows = q_in.shape[0]
@@ -57,6 +61,22 @@
     groups = width // HD
     factor = HD ** -0.5 * math.log2(math.e)
 
+    barrier = pltpu.get_barrier_semaphore()
+
+    @pl.when(me > 0)
+    def _():
+        pl.semaphore_wait(barrier, 1)
+
+    @pl.when(me < n - 1)
+    def _():
+        pl.semaphore_signal(barrier, inc=1, device_id={"head": lax.rem(me + 1, n)}, device_id_type=MESH)
+
+    for w in range(n - 1):
+
+        @pl.when(w < me)
+        def _(w=w):
+            pl.semaphore_signal(in_sem.at[me], inc=1, device_id={"head": w}, device_id_type=MESH)
+
     own = []
     for a, (src, dst, h, w) in enumerate(
         ((t_in, t_buf, trows, twidth), (q_in, q_buf, rows, width), (k_in, k_buf, rows, width), (v_in, v_buf, rows, width))
@@ -70,22 +90,6 @@
         own.append(copy)
     g_copy = pltpu.make_async_copy(g_in, g_buf, local_sem.at[4])
     g_copy.start()
-
-    barrier = pltpu.get_barrier_semaphore()
-
-    @pl.when(me > 0)
-    def _():
-        pl.semaphore_wait(barrier, 1)
-
-    @pl.when(me < n - 1)
-    def _():
-        pl.semaphore_signal(barrier, inc=1, device_id={"head": lax.rem(me + 1, n)}, device_id_type=MESH)
-
-    for w in range(n - 1):
-
-        @pl.when(w < me)
-        def _(w=w):
-            pl.semaphore_signal(in_sem.at[me], inc=1, device_id={"head": w}, device_id_type=MESH)
 
     arrays = ((t_in, t_buf, trows, twidth), (q_in, q_buf, rows, width), (k_in, k_buf, rows, width), (v_in, v_buf, rows, width))
 
@@ -109,9 +113,36 @@
         block_copy(0, me, to, to).start()
         block_copy(1, me, to, to).start()
 
-    for a in (2, 3):
-        for to in peers(n, me, near_first):
-            block_copy(a, me, to, to).start()
+    half, hop = n // 2, n // 4
+    facing = lax.rem(me + half, n)
+
+    def to_relay(via, target):
+        return pltpu.make_async_remote_copy(
+            src_ref=v_in.at[:, pl.ds(pl.multiple_of(target * width, width), width)],
+            dst_ref=relay_buf,
+            send_sem=send_sem.at[3, target],
+            recv_sem=relay_sem,
+            device_id={"head": via},
+            device_id_type=MESH,
+        )
+
+    def from_relay(source, target):
+        return pltpu.make_async_remote_copy(
+            src_ref=relay_buf,
+            dst_ref=v_buf.at[pl.ds(pl.multiple_of(source * rows, rows), rows), :],
+            send_sem=pass_sem,
+            recv_sem=recv_sem.at[3, source],
+            device_id={"head": target},
+            device_id_type=MESH,
+        )
+
+    @pl.when(me < half)
+    def _():
+        to_relay(me + hop, facing).start()
+
+    relays = jnp.logical_and(me >= hop, me < hop + half)
+    for to in peers(n, me, near_first):
+        block_copy(2, me, to, to).start()
 
     others = [lax.rem(me + d, n) for d in range(1, n)]
 
@@ -123,6 +154,17 @@
     g_copy.wait()
     arrive(0)
     arrive(1)
+
+    @pl.when(relays)
+    def _():
+        to_relay(me + hop, me + hop).wait_recv()
+        from_relay(me - hop, me + hop).start()
+
+    for to in peers(n, me, ascending):
+
+        @pl.when(jnp.logical_or(me >= half, to != facing))
+        def _():
+            block_copy(3, me, to, to).start()
 
     dk_acc[...] = jnp.zeros_like(dk_acc)
     dv_acc[...] = jnp.zeros_like(dv_acc)
@@ -167,7 +209,8 @@
             device_id_type=MESH,
         )
 
-    for to in peers(n, me, near_first):
+    for to in peers(n, me, ascending):
+
         grad_copy(me, to, to).start()
 
     arrive(2)
@@ -203,6 +246,11 @@
     lax.fori_loop(0, length // block, value_step, 0)
 
     own_grad.wait()
+
+    @pl.when(relays)
+    def _():
+        from_relay(me - hop, me + hop).wait_send()
+
     for other in others:
         for a in range(4):
             block_copy(a, me, other, other).wait_send()
@@ -213,10 +261,12 @@
 
 
 def place(a_in, b_in, a_out, b_out, sems):
-    copies = [
-        pltpu.make_async_copy(a_in, a_out, sems.at[0]),
-        pltpu.make_async_copy(b_in, b_out, sems.at[1]),
-    ]
+    copies = []
+    for src, dst, pieces in ((a_in, a_out, 4), (b_in, b_out, 2)):
+        step = src.shape[0] // pieces
+        for i in range(pieces):
+            at = pl.ds(i * step, step)
+            copies.append(pltpu.make_async_copy(src.at[at, :], dst.at[at, :], sems.at[len(copies)]))
     for copy in copies:
         copy.start()
     for copy in copies:
@@ -250,6 +300,7 @@
             pltpu.VMEM((groups, text, HD), F32),
             pltpu.VMEM((groups, text, HD), F32),
             pltpu.VMEM((text, twidth), BF16),
+            pltpu.VMEM((rows, width), BF16),
             pltpu.SemaphoreType.DMA((4, n)),
             pltpu.SemaphoreType.DMA((4, n)),
             pltpu.SemaphoreType.DMA((6,)),
@@ -257,6 +308,8 @@
             pltpu.SemaphoreType.DMA((n,)),
             pltpu.SemaphoreType.DMA((n,)),
             pltpu.SemaphoreType.REGULAR((n,)),
+            pltpu.SemaphoreType.DMA,
+            pltpu.SemaphoreType.DMA,
         ],
         compiler_params=pltpu.CompilerParams(
             collective_id=0, has_side_effects=True, vmem_limit_bytes=40 * 2**20
@@ -270,7 +323,7 @@
         ),
         in_specs=[pl.BlockSpec(memory_space=pl.ANY)] * 2,
         out_specs=(pl.BlockSpec(memory_space=pltpu.HBM),) * 2,
-        scratch_shapes=[pltpu.SemaphoreType.DMA((2,))],
+        scratch_shapes=[pltpu.SemaphoreType.DMA((6,))],
     )(*(pltpu.with_memory_space_constraint(x, pltpu.VMEM) for x in (attended, grad)))
     return attended[None], grad[None]
 

time: 119 us -> 117 us (0.983)
  Pallas kernels: 118 us -> 115 us
    pallas_call x1, Pallas kernels: 117 us -> 114 us  [per_device(): pl.pallas_call(functools.partial(kernel, n), out_shape=(pltpu.VMEM((lengt...]
where the time goes in v3:
time: 117 us; the launch traced here: 116 us
  Pallas kernels  115 us (98%)
    pallas_call x1, Pallas kernels, per_device(): pl.pallas_call(functools.partial(kernel, n), out_shape=(pltpu.VMEM((lengt...  114 us

profile of v3, /device:TPU:56, one launch (start us, length us, event | category | flops | bytes accessed | tf_op | source)
XLA Modules:
  0.0 115.9 jit_solution(10503516210344645777)
XLA Ops:
  0.6 114.2 %shard_map.68 = (bf16[1536,256]{1,0:T(8,128)(2,1)S(1)}, bf16[32,6144]{1,0:T(8,128)(2,1)S(1)}) custom-call(bf16[128,3072]{1,0:T(8,128)(2,1)} %bitcast.7, bf16[128,3072]{1,0:T(8,128)(2,1)} %bitcast.8, bf16[128,3072]{1,0:T(8,128)(2,1)} %bitcast.9, bf16[32,6144]{1,0:T(8,128)(2,1)} %bitcast.11, bf16[1536,256]{1,0:T(8,128)(2,1)} %bitcast.10), custom_call_target="tpu_custom_call" | custom-call | tf_op jit(solution)/shard_map/pallas_call | solution.py:283
  114.8 1.1 shard_map.69

commit v4 on v3

--- a/solution.py
+++ b/solution.py
@@ -116,33 +116,37 @@
     half, hop = n // 2, n // 4
     facing = lax.rem(me + half, n)
 
-    def to_relay(via, target):
+    def to_relay(a, via, target):
         return pltpu.make_async_remote_copy(
-            src_ref=v_in.at[:, pl.ds(pl.multiple_of(target * width, width), width)],
-            dst_ref=relay_buf,
-            send_sem=send_sem.at[3, target],
-            recv_sem=relay_sem,
+            src_ref=arrays[a][0].at[:, pl.ds(pl.multiple_of(target * width, width), width)],
+            dst_ref=relay_buf.at[a - 2],
+            send_sem=send_sem.at[a, target],
+            recv_sem=relay_sem.at[a - 2],
             device_id={"head": via},
             device_id_type=MESH,
         )
 
-    def from_relay(source, target):
+    def from_relay(a, source, target):
         return pltpu.make_async_remote_copy(
-            src_ref=relay_buf,
-            dst_ref=v_buf.at[pl.ds(pl.multiple_of(source * rows, rows), rows), :],
-            send_sem=pass_sem,
-            recv_sem=recv_sem.at[3, source],
+            src_ref=relay_buf.at[a - 2],
+            dst_ref=arrays[a][1].at[pl.ds(pl.multiple_of(source * rows, rows), rows), :],
+            send_sem=pass_sem.at[a - 2],
+            recv_sem=recv_sem.at[a, source],
             device_id={"head": target},
             device_id_type=MESH,
         )
 
     @pl.when(me < half)
     def _():
-        to_relay(me + hop, facing).start()
+        for a in (2, 3):
+            to_relay(a, me + hop, facing).start()
 
     relays = jnp.logical_and(me >= hop, me < hop + half)
     for to in peers(n, me, near_first):
-        block_copy(2, me, to, to).start()
+
+        @pl.when(jnp.logical_or(me >= half, to != facing))
+        def _():
+            block_copy(2, me, to, to).start()
 
     others = [lax.rem(me + d, n) for d in range(1, n)]
 
@@ -157,8 +161,9 @@
 
     @pl.when(relays)
     def _():
-        to_relay(me + hop, me + hop).wait_recv()
-        from_relay(me - hop, me + hop).start()
+        for a in (2, 3):
+            to_relay(a, me + hop, me + hop).wait_recv()
+            from_relay(a, me - hop, me + hop).start()
 
     for to in peers(n, me, ascending):
 
@@ -249,7 +254,8 @@
 
     @pl.when(relays)
     def _():
-        from_relay(me - hop, me + hop).wait_send()
+        for a in (2, 3):
+            from_relay(a, me - hop, me + hop).wait_send()
 
     for other in others:
         for a in range(4):
@@ -300,7 +306,7 @@
             pltpu.VMEM((groups, text, HD), F32),
             pltpu.VMEM((groups, text, HD), F32),
             pltpu.VMEM((text, twidth), BF16),
-            pltpu.VMEM((rows, width), BF16),
+            pltpu.VMEM((2, rows, width), BF16),
             pltpu.SemaphoreType.DMA((4, n)),
             pltpu.SemaphoreType.DMA((4, n)),
             pltpu.SemaphoreType.DMA((6,)),
@@ -308,8 +314,8 @@
             pltpu.SemaphoreType.DMA((n,)),
             pltpu.SemaphoreType.DMA((n,)),
             pltpu.SemaphoreType.REGULAR((n,)),
-            pltpu.SemaphoreType.DMA,
-            pltpu.SemaphoreType.DMA,
+            pltpu.SemaphoreType.DMA((2,)),
+            pltpu.SemaphoreType.DMA((2,)),
         ],
         compiler_params=pltpu.CompilerParams(
             collective_id=0, has_side_effects=True, vmem_limit_bytes=40 * 2**20

time: 117 us -> 120 us (1.026); the launches traced: 116 us -> 118 us
  Pallas kernels: 115 us -> 117 us
    pallas_call x1, Pallas kernels: 114 us -> 116 us  [per_device(): pl.pallas_call(functools.partial(kernel, n), out_shape=(pltpu.VMEM((lengt...]
where the time goes in v4:
time: 120 us; the launch traced here: 118 us
  Pallas kernels  117 us (98%)
    pallas_call x1, Pallas kernels, per_device(): pl.pallas_call(functools.partial(kernel, n), out_shape=(pltpu.VMEM((lengt...  116 us

profile of v4, /device:TPU:56, one launch (start us, length us, event | category | flops | bytes accessed | tf_op | source)
XLA Modules:
  0.0 117.5 jit_solution(15593163219879741993)
XLA Ops:
  0.6 115.9 %shard_map.68 = (bf16[1536,256]{1,0:T(8,128)(2,1)S(1)}, bf16[32,6144]{1,0:T(8,128)(2,1)S(1)}) custom-call(bf16[128,3072]{1,0:T(8,128)(2,1)} %bitcast.7, bf16[128,3072]{1,0:T(8,128)(2,1)} %bitcast.8, bf16[128,3072]{1,0:T(8,128)(2,1)} %bitcast.9, bf16[32,6144]{1,0:T(8,128)(2,1)} %bitcast.11, bf16[1536,256]{1,0:T(8,128)(2,1)} %bitcast.10), custom_call_target="tpu_custom_call" | custom-call | tf_op jit(solution)/shard_map/pallas_call | solution.py:289
  116.5 1.1 shard_map.69
